TPU v7x, 256 devices: a whole 4x4x8 slice. The times are simulated.
256 devices in a mesh: dp: 8 (over z_hi, y), mp: 32 (over x, z_lo, core).
Axes of the slice: x: 4, y: 4, z: 8 (z_hi: 2, z_lo: 4; z = z_hi * 4 + z_lo), core: 2. Of those that a mesh axis runs over, the one named last changes fastest.
Arguments:
- tokens: bfloat16 [8192, 2560], P('dp'), may hold values from -6 to 6
- cotangent: bfloat16 [8192, 10240], P('dp', 'mp'), may hold values from -0.0625 to 0.0625
- saved_panels: bfloat16 [2048, 8192], P(None, 'mp'), may hold values from -0.125 to 0.125
- owners: int32 [32, 2], replicated, may hold values from 0 to 7, as said below
- row_growth: bfloat16 [2560, 2048], P(None, 'dp'), may hold values from -0.125 to 0.125
- col_growth: bfloat16 [10240, 8192], P('mp', 'dp'), may hold values from -0.0625 to 0.0625
Outputs:
- grown_out: bfloat16 [8192, 10240], P('dp', 'mp')
- grad_grown: float32 [2560, 10240], P('dp', 'mp')
- grad_row_growth: float32 [2560, 2048], P('mp', 'dp')
- grad_col_growth: float32 [10240, 8192], P('mp', 'dp')
Inputs may be any that keep to these rules, and one draw needn't show every extreme that they name: `owners`: column 0 is a rank below 8, column 1 a section below 4; every pair of rank and section names exactly one panel.
All inputs are finite; a program needn't handle non-finite values.
Results may differ from a plain program's by a relative error of at most 0.006.
Values may be sent and summed in bfloat16 or wider, within the bound.
No kernel may reach another device: no remote copies, remote signals or barrier semaphores. Data moves between devices by JAX's collectives and lax.ppermute only.
A program may use at most 128 MiB of HBM per device.

v0:
```python
import jax
import jax.numpy as jnp
from jax import lax
from jax.sharding import PartitionSpec as P

SECTIONS = 4


def broadcast(block, axis, source):
    block = jnp.where(lax.axis_index(axis) == source, block, jnp.zeros_like(block))
    return lax.psum(block, axis)


def shards(tokens, cotangent, saved_panels, owners, row_growth, col_growth):
    dp_count = lax.axis_size("dp")
    mp_count = lax.axis_size("mp")
    dp_index = lax.axis_index("dp")
    per_part = mp_count // dp_count
    slot_of = owners[:, 1] * (mp_count // SECTIONS) + owners[:, 0]
    received = []
    for within in range(per_part):
        root_slot = slot_of[dp_index * per_part + within]
        received.append(broadcast(saved_panels, "mp", root_slot))
    part_weight = jnp.concatenate(received, axis=1)
    trailing = (((1,), (1,)), ((), ()))
    leading = (((0,), (0,)), ((), ()))
    inner = lax.psum_scatter(
        lax.dot_general(part_weight, col_growth, trailing, preferred_element_type=jnp.float32),
        "dp",
        scatter_dimension=0,
        tiled=True,
    ).astype(jnp.bfloat16)
    new_rows = row_growth.shape[0] // dp_count
    grown_term = jnp.dot(row_growth, inner, preferred_element_type=jnp.float32)
    grad_term = lax.dot_general(tokens, cotangent, leading, preferred_element_type=jnp.float32)
    grown_sum, grad_sum = lax.psum((grown_term, grad_term), "dp")
    grown = grown_sum.astype(jnp.bfloat16)
    grad_rounded = grad_sum.astype(jnp.bfloat16)
    grad_block = lax.dynamic_slice_in_dim(grad_sum, dp_index * new_rows, new_rows, 0)
    grown_out = jnp.dot(tokens, grown, preferred_element_type=jnp.float32).astype(jnp.bfloat16)
    back_inner = lax.dot_general(
        row_growth, grad_rounded, leading, preferred_element_type=jnp.float32
    ).astype(jnp.bfloat16)
    grad_col = lax.dot_general(
        lax.all_gather(back_inner, "dp", axis=0, tiled=True),
        part_weight,
        leading,
        preferred_element_type=jnp.float32,
    )
    grad_row = lax.psum_scatter(
        lax.dot_general(grad_rounded, inner, trailing, preferred_element_type=jnp.float32),
        "mp",
        scatter_dimension=0,
        tiled=True,
    )
    return (grown_out, grad_block, grad_row, grad_col)


def solution(mesh):
    in_specs = (P("dp", None), P("dp", "mp"), P(None, "mp"), P(), P(None, "dp"), P("mp", "dp"))
    out_specs = (P("dp", "mp"), P("dp", "mp"), P("mp", "dp"), P("mp", "dp"))
    return jax.shard_map(shards, mesh=mesh, in_specs=in_specs, out_specs=out_specs, check_vma=False)
```

profile of v0, /device:TPU:30, one launch (start us, length us, event | category | flops | bytes accessed | tf_op | source)
XLA Modules:
  0.0 842.7 jit_solution(17480406401961617846)
XLA Ops:
  7.2 0.8 slice_add_fusion
  8.0 0.6 constant_dynamic-slice_fusion.1
  11.2 3.4 broadcast_select_fusion
  14.6 0.0 all-reduce.5.cloned.1.call-start
  14.7 1.0 copy-done.5
  15.7 6.1 fusion.16
  21.9 274.1 %all-reduce.7.cloned.1.call-done = (bf16[2048,256]{1,0:T(8,128)(2,1)}, bf16[2048,256]{1,0:T(8,128)(2,1)}, bf16[2048,256]{1,0:T(8,128)(2,1)}, bf16[2048,256]{1,0:T(8,128)(2,1)}) async-done(((bf16[2048,256]{1,0:T(8,128)(2,1)}, bf16[2048,256]{1,0:T(8,128)(2,1)}, bf16[2048,256]{1,0:T(8,128)(2,1)}, bf16[2048,256]{1,0:T(8,128)(2,1)}), (bf16[2048,256]{1,0:T(8,128)(2,1)}, bf16[2048,256]{1,0:T(8,128)(2,1)}, ...) | async-done | bytes 4194320 | tf_op jit(solution)/shard_map/psum | solution.py:11
  296.0 1.5 constant_dynamic-update-slice_fusion.3
  297.5 1.4 constant_dynamic-update-slice_fusion.2
  298.9 0.1 constant_dynamic-update-slice_fusion.1
  299.1 0.1 constant_dynamic-update-slice_fusion
  299.2 2.0 copy-done.4
  301.2 3.1 fusion.14
  304.4 175.3 %all-reduce.5.cloned.1.call-done = f32[2560,320]{0,1:T(8,128)} async-done(((f32[2560,320]{0,1:T(8,128)}), f32[2560,320]{0,1:T(8,128)}) %all-reduce.5.cloned.1.call-update) | async-done | bytes 3276816 | tf_op jit(solution)/shard_map/psum | solution.py:36
  479.8 3.2 fusion.8
  483.0 101.9 %reduce-scatter.3.cloned.1.call-done = f32[256,320]{0,1:T(8,128)} async-done(((f32[2048,320]{0,1:T(8,128)}), f32[256,320]{0,1:T(8,128)}) %reduce-scatter.3.cloned.1.call-update) | async-done | bytes 327696 | tf_op jit(solution)/shard_map/reduce_scatter | solution.py:27
  584.9 4.4 fusion.10
  589.3 1.3 constant_dynamic-slice_fusion
  590.6 1.0 copy.10
  591.6 57.7 %all-gather.2.cloned.1.call-done = bf16[2048,320]{0,1:T(8,128)(2,1)} async-done(((bf16[256,320]{0,1:T(8,128)(2,1)}), bf16[2048,320]{0,1:T(8,128)(2,1)}) %all-gather.2.cloned.1.call-update) | async-done | bytes 1310736 | tf_op jit(solution)/shard_map/all_gather | solution.py:45
  649.3 5.2 fusion.15
  654.5 2.3 convolution_bitcast_fusion
  656.8 174.1 %all-reduce.8 = bf16[2560,320]{0,1:T(8,128)(2,1)S(1)} all-reduce(f32[2560,320]{0,1:T(8,128)} %convolution_bitcast_fusion), channel_id=1, replica_groups=mesh['dp'=8,'mp'=32] {'dp'}, use_global_device_ids=true, to_apply=%region_5.6 | all-reduce | flops 819200 | bytes 4915200 | tf_op jit(solution)/shard_map/psum | solution.py:36
  830.9 5.2 fusion.5
  (22 shorter events, 0.3 us)
Async XLA Ops:
  7.2 472.6 %copy-start = (bf16[2560,256]{1,0:T(8,128)(2,1)S(1)}, bf16[2560,256]{1,0:T(8,128)(2,1)}, u32[]{:S(2)}) copy-start(bf16[2560,256]{1,0:T(8,128)(2,1)} %param.10) | copy-start | bytes 3932164
  7.2 288.8 %all-reduce.7.cloned.1.call-start = ((), (), s32[]{:S(2)}) async-start(), calls=%async_computation.6 | async-start | bytes 8388608 | tf_op jit(solution)/shard_map/psum | solution.py:11
  14.6 1.1 copy-start.5
  14.6 465.1 %all-reduce.5.cloned.1.call-start = ((), (), s32[]{:S(2)}) async-start(), calls=%async_computation.3 | async-start | bytes 6553600 | tf_op jit(solution)/shard_map/psum | solution.py:36
  21.8 563.1 %reduce-scatter.3.cloned.1.call-start = ((), (), s32[]{:S(2)}) async-start(), calls=%async_computation.2 | async-start | bytes 2949120 | tf_op jit(solution)/shard_map/reduce_scatter | solution.py:27
  296.0 3.0 copy-start.3
  296.0 3.1 copy-start.2
  297.5 3.7 copy-start.6
  299.2 2.0 copy-start.4
  304.4 345.0 %all-gather.2.cloned.1.call-start = ((), (), s32[]{:S(2)}) async-start(), calls=%async_computation.5 | async-start | bytes 1474560 | tf_op jit(solution)/shard_map/all_gather | solution.py:45
  483.0 353.2 %reduce-scatter.5.cloned.1.call-start = ((), (), s32[]{:S(2)}) async-start(), calls=%async_computation.4 | async-start | bytes 2703360 | tf_op jit(solution)/shard_map/reduce_scatter | solution.py:50
  591.6 62.9 %copy-start.1 = (f32[256,320]{0,1:T(8,128)S(1)}, f32[256,320]{0,1:T(8,128)}, u32[]{:S(2)}) copy-start(f32[256,320]{0,1:T(8,128)} %reduce-scatter.3.cloned.1.call-done) | copy-start | bytes 983044
Sparse Core Ops, SparseCore 0:
  14.7 281.1 all-reduce.6
  298.6 181.0 all-reduce.4
  484.4 100.4 reduce-scatter.2
  588.1 61.1 all-gather.1
  652.4 161.9 reduce-scatter.4
where the time goes:
time: 843 us
  waiting for transfers between devices  609 us (72%)
  blocking collectives  174 us (21%)
  matrix products  29.5 us (3%)
  between operations  16.5 us (2%)
  local copies, waits for them, and re-layouts  9.08 us (1%)
    psum x1, waiting for transfers between devices, broadcast(): return lax.psum(block, axis)  274 us
    psum x1, waiting for transfers between devices, shards(): grown_sum, grad_sum = lax.psum((grown_term, grad_term), 'dp')  175 us
    psum x1, blocking collectives, shards(): grown_sum, grad_sum = lax.psum((grown_term, grad_term), 'dp')  174 us
    reduce_scatter x1, waiting for transfers between devices, shards(): lax.psum_scatter(lax.dot_general(part_weight, col_growth, trailing, prefe...  102 us
    all_gather x1, waiting for transfers between devices, shards(): lax.all_gather(back_inner, 'dp', axis=0, tiled=True)  57.7 us
  transfers between devices with their start and end apart: 5, of which 4 were waited for; matrix products, arithmetic and copies ran while one was open for 4% of the time, Pallas kernels for 0%

commit v1 on v0

v1 whole, which is shorter than its diff:
```python
import jax
import jax.numpy as jnp
from jax import lax
from jax.sharding import PartitionSpec as P

SECTIONS = 4
ZH, NY = 2, 4
NX, NZ, NC = 4, 4, 2
Y_GROUPS = [[h * NY + y for y in range(NY)] for h in range(ZH)]
X_GROUPS = [[(x * NZ + z) * NC + c for x in range(NX)] for z in range(NZ) for c in range(NC)]
Z_GROUPS = [[(x * NZ + z) * NC + c for z in range(NZ)] for x in range(NX) for c in range(NC)]
SWAP_ZH = [(i, (i + NY) % (ZH * NY)) for i in range(ZH * NY)]
SWAP_CORE = [(m, m ^ 1) for m in range(NX * NZ * NC)]
BF, F32 = jnp.bfloat16, jnp.float32


def dot(a, b, dims, kind=F32):
    return lax.dot_general(a, b, (dims, ((), ())), preferred_element_type=F32).astype(kind)


def exchange(blocks, axis, groups=None):
    return lax.all_to_all(blocks, axis, 0, 0, axis_index_groups=groups)


def gather(block, axis, groups, count):
    return exchange(jnp.broadcast_to(block[None], (count,) + block.shape), axis, groups)


def pick(blocks, index):
    return lax.dynamic_index_in_dim(blocks, index, 0, keepdims=False)


def reduce_rows(term, z_hi):
    blocks = term.reshape(ZH, NY, -1, term.shape[1]).transpose(1, 0, 2, 3).astype(BF)
    part = exchange(blocks, "dp", Y_GROUPS).astype(F32).sum(axis=0)
    other = lax.ppermute(pick(part, 1 - z_hi).astype(BF), "dp", SWAP_ZH)
    return pick(part, z_hi) + other.astype(F32)


def gather_rows(block, z_hi):
    other = lax.ppermute(block, "dp", SWAP_ZH)
    pair = jnp.where(z_hi == 0, jnp.stack([block, other]), jnp.stack([other, block]))
    return gather(pair, "dp", Y_GROUPS, NY)


def source_part(saved, slot_of, z_hi, y):
    width = saved.shape[1]
    sub = saved.shape[0] // (NX * NZ * NC * NY)
    rows = saved.reshape(NC, NX, NZ, NY, sub, width)
    mine = lax.dynamic_index_in_dim(rows, y, 3, keepdims=False)
    mine = mine.transpose(1, 2, 0, 3, 4).reshape(NX * NZ * NC, sub, width)
    slots = exchange(mine, "mp")
    panels = jnp.take(slots, slot_of, axis=0).reshape(ZH, NY, -1, sub, width)
    parts = exchange(pick(panels, z_hi), "dp", Y_GROUPS)
    chunk = parts.transpose(0, 2, 1, 3).reshape(NY * sub, -1)
    plane = gather(chunk, "mp", Z_GROUPS, NZ)
    plane = gather(plane.reshape(-1, chunk.shape[1]), "mp", X_GROUPS, NX)
    half = plane.reshape(-1, chunk.shape[1])
    other = lax.ppermute(half, "mp", SWAP_CORE)
    core = lax.axis_index("mp") % NC
    return jnp.where(
        core == 0, jnp.concatenate([half, other]), jnp.concatenate([other, half])
    )


def shards(tokens, cotangent, saved_panels, owners, row_growth, col_growth):
    dp_index, mp_index = lax.axis_index("dp"), lax.axis_index("mp")
    mp_count = lax.axis_size("mp")
    z_hi, y = dp_index // NY, dp_index % NY
    slot_of = owners[:, 1] * (mp_count // SECTIONS) + owners[:, 0]
    old = row_growth.shape[1]
    hidden = cotangent.shape[1]

    strip = old // mp_count
    strips = pick(row_growth.T.reshape(mp_count, strip, -1), mp_index)
    strips = gather(strips, "dp", None, ZH * NY).reshape(ZH * NY * strip, -1)
    mixed = dot(strips, tokens, ((1,), (1,)), BF)
    mixed = lax.all_gather(mixed, "mp", axis=0, tiled=True)

    part_weight = source_part(saved_panels, slot_of, z_hi, y)

    grad = reduce_rows(dot(tokens, cotangent, ((0,), (0,))), z_hi)
    grad_all = gather_rows(grad.astype(BF), z_hi).reshape(-1, hidden)
    ordered_growth = (
        row_growth.reshape(ZH, NY, -1, old).transpose(1, 0, 2, 3).reshape(-1, old)
    )
    back = gather_rows(dot(ordered_growth, grad_all, ((0,), (0,)), BF), z_hi)
    back = back.transpose(1, 0, 2, 3).reshape(-1, hidden)
    grad_col = dot(back, part_weight, ((0,), (0,)))

    inner = reduce_rows(dot(part_weight, col_growth, ((1,), (1,))), z_hi).astype(BF)
    inner_all = gather_rows(inner, z_hi)

    grow = dot(grad_all, inner, ((1,), (1,)))
    rows = grow.shape[0] // mp_count
    grow = grow.reshape(NY, ZH, -1, rows, old).transpose(1, 0, 2, 3, 4)
    grow = grow.reshape(NX * NZ, NC, rows, old)
    core = mp_index % NC
    keep = lax.dynamic_index_in_dim(grow, core, 1, keepdims=False)
    give = lax.dynamic_index_in_dim(grow, 1 - core, 1, keepdims=False)
    keep = keep + lax.ppermute(give.astype(BF), "mp", SWAP_CORE).astype(F32)
    keep = keep.reshape(NX, NZ, rows, old).astype(BF)
    keep = exchange(keep, "mp", X_GROUPS).astype(F32).sum(axis=0)
    grad_row = exchange(keep, "mp", Z_GROUPS).sum(axis=0)

    inner_all = inner_all.transpose(1, 0, 2, 3).reshape(ZH * NY, mp_count, strip, hidden)
    inner_all = inner_all.transpose(1, 0, 2, 3).reshape(-1, hidden)
    grown_out = dot(mixed, inner_all, ((0,), (0,)), BF)
    return (grown_out, grad, grad_row, grad_col)


def solution(mesh):
    in_specs = (P("dp", None), P("dp", "mp"), P(None, "mp"), P(), P(None, "dp"), P("mp", "dp"))
    out_specs = (P("dp", "mp"), P("dp", "mp"), P("mp", "dp"), P("mp", "dp"))
    return jax.shard_map(shards, mesh=mesh, in_specs=in_specs, out_specs=out_specs, check_vma=False)
```

time: 843 us -> 310 us (0.37)
  waiting for transfers between devices: 609 us -> 110 us
  blocking collectives: 174 us -> 14 us
  starting transfers between devices: 0.21 us -> 90.2 us
  local copies, waits for them, and re-layouts: 9.08 us -> 38.8 us
    psum x2 -> x0, waiting for transfers between devices: 449 us -> none  [the longest x1 274 us: broadcast(): return lax.psum(block, axis)]
    psum x1 -> x0, blocking collectives: 174 us -> none  [shards(): grown_sum, grad_sum = lax.psum((grown_term, grad_term), 'dp')]
    reduce_scatter x2 -> x0, waiting for transfers between devices: 102 us -> none  [the longest x1 102 us: shards(): lax.psum_scatter(lax.dot_general(part_weight, col_growth, trailing, prefe...]
    all_to_all x0 -> x11, starting transfers between devices: none -> 71.7 us  [exchange(): return lax.all_to_all(blocks, axis, 0, 0, axis_index_groups=groups)]
    all_to_all x0 -> x11, waiting for transfers between devices: none -> 70.4 us  [exchange(): return lax.all_to_all(blocks, axis, 0, 0, axis_index_groups=groups)]
    all_gather x1, waiting for transfers between devices: 57.7 us -> 0.01 us  [shards(): mixed = lax.all_gather(mixed, 'mp', axis=0, tiled=True)]
    ppermute x0 -> x7, waiting for transfers between devices: none -> 39.8 us  [the longest x3 19.1 us: gather_rows(): other = lax.ppermute(block, 'dp', SWAP_ZH)]
    ppermute x0 -> x7, starting transfers between devices: none -> 18.5 us  [the longest x3 10.3 us: gather_rows(): other = lax.ppermute(block, 'dp', SWAP_ZH)]
  transfers between devices with their start and end apart: 5 -> 19, of which waited for: 4 -> 13; matrix products, arithmetic and copies ran while one was open for 4% -> 22% of each run, Pallas kernels for 0% -> 0%
where the time goes in v1:
time: 310 us; the launch traced here: 307 us
  waiting for transfers between devices  110 us (35%)
  starting transfers between devices  90.2 us (29%)
  local copies, waits for them, and re-layouts  38.8 us (13%)
  matrix products  30 us (10%)
  between operations  14.4 us (5%)
  blocking collectives  14 us (5%)
  other arithmetic  9.31 us (3%)
    all_to_all x11, starting transfers between devices, exchange(): return lax.all_to_all(blocks, axis, 0, 0, axis_index_groups=groups)  71.7 us
    all_to_all x11, waiting for transfers between devices, exchange(): return lax.all_to_all(blocks, axis, 0, 0, axis_index_groups=groups)  70.4 us
    dot_general x7, matrix products, dot(): lax.dot_general(a, b, (dims, ((), ())), preferred_element_type=F32)  30 us
    ppermute x3, waiting for transfers between devices, gather_rows(): other = lax.ppermute(block, 'dp', SWAP_ZH)  19.1 us
    ppermute x2, waiting for transfers between devices, reduce_rows(): other = lax.ppermute(pick(part, 1 - z_hi).astype(BF), 'dp', SWAP_ZH)  18.5 us
    all_to_all x1, blocking collectives, exchange(): return lax.all_to_all(blocks, axis, 0, 0, axis_index_groups=groups)  14 us
    convert_element_type x4, local copies, waits for them, and re-layouts, reduce_rows(): term.reshape(ZH, NY, -1, term.shape[1]).transpose(1, 0, 2, 3).astype(BF)  12.5 us
    ppermute x3, starting transfers between devices, gather_rows(): other = lax.ppermute(block, 'dp', SWAP_ZH)  10.3 us
  transfers between devices with their start and end apart: 19, of which 13 were waited for; matrix products, arithmetic and copies ran while one was open for 22% of the time, Pallas kernels for 0%

profile of v1, /device:TPU:30, one launch (start us, length us, event | category | flops | bytes accessed | tf_op | source)
XLA Modules:
  0.0 306.9 jit_solution(3369572211451372550)
XLA Ops:
  9.2 9.0 %all-to-all-start.1 = ((bf16[32,16,256]{2,1,0:T(8,128)(2,1)}), bf16[32,16,256]{2,1,0:T(8,128)(2,1)S(1)}, u32[]{:S(2)}, u32[]{:S(2)}) async-start(bf16[32,16,256]{2,1,0:T(8,128)(2,1)} %bitcast.7), calls=%async_computation.1 | async-start | bytes 524288 | tf_op jit(solution)/shard_map/all_to_all | solution.py:22
  19.9 7.2 %all-to-all-done.1 = bf16[32,16,256]{2,1,0:T(8,128)(2,1)S(1)} async-done(((bf16[32,16,256]{2,1,0:T(8,128)(2,1)}), bf16[32,16,256]{2,1,0:T(8,128)(2,1)S(1)}, u32[]{:S(2)}, u32[]{:S(2)}) %all-to-all-start.1) | async-done | bytes 262176 | tf_op jit(solution)/shard_map/all_to_all | solution.py:22
  38.0 8.4 %all-to-all-start = ((bf16[8,8,2560]{2,1,0:T(8,128)(2,1)}), bf16[8,8,2560]{2,1,0:T(8,128)(2,1)S(1)}, u32[]{:S(2)}, u32[]{:S(2)}) async-start(bf16[8,8,2560]{2,1,0:T(8,128)(2,1)} %broadcast_in_dim.53), calls=%async_computation | async-start | bytes 655360 | tf_op jit(solution)/shard_map/all_to_all | solution.py:22
  46.5 10.5 %all-to-all-done = bf16[8,8,2560]{2,1,0:T(8,128)(2,1)S(1)} async-done(((bf16[8,8,2560]{2,1,0:T(8,128)(2,1)}), bf16[8,8,2560]{2,1,0:T(8,128)(2,1)S(1)}, u32[]{:S(2)}, u32[]{:S(2)}) %all-to-all-start) | async-done | bytes 327712 | tf_op jit(solution)/shard_map/all_to_all | solution.py:22
  57.1 14.0 %all_to_all.60 = bf16[4,64,1024]{2,1,0:T(8,128)(2,1)S(1)} all-to-all(bf16[4,64,1024]{2,1,0:T(8,128)(2,1)S(1)} %broadcast_in_dim.58), channel_id=1, replica_groups={{0,2,4,6},{1,3,5,7},{8,10,12,14},{9,11,13,15},{16,18,20,22},{17,19,21,2..., dimensions={0} | all-to-all | bytes 1048576 | tf_op jit(solution)/shard_map/all_to_all | solution.py:22
  72.7 8.2 %all-to-all-start.4 = ((bf16[4,256,1024]{2,1,0:T(8,128)(2,1)}), bf16[4,256,1024]{2,1,0:T(8,128)(2,1)}, u32[]{:S(2)}, u32[]{:S(2)}) async-start(bf16[4,256,1024]{2,1,0:T(8,128)(2,1)} %broadcast_in_dim.60), calls=%async_computation.4 | async-start | bytes 4194304 | tf_op jit(solution)/shard_map/all_to_all | solution.py:22
  80.9 5.5 %convolution_convert_fusion = bf16[2560,320]{0,1:T(8,128)(2,1)} fusion(bf16[1024,320]{0,1:T(8,128)(2,1)S(1)} %copy-done.6, bf16[1024,2560]{1,0:T(8,128)(2,1)} %param.6), kind=kOutput, calls=%fused_computation.2 | convolution fusion | flops 1678540800 | bytes 7536640 | tf_op jit(solution)/shard_map/dot_general | solution.py:18
  93.6 10.5 %all-to-all-done.4 = bf16[4,256,1024]{2,1,0:T(8,128)(2,1)} async-done(((bf16[4,256,1024]{2,1,0:T(8,128)(2,1)}), bf16[4,256,1024]{2,1,0:T(8,128)(2,1)}, u32[]{:S(2)}, u32[]{:S(2)}) %all-to-all-start.4) | async-done | bytes 2097184 | tf_op jit(solution)/shard_map/all_to_all | solution.py:22
  104.1 5.3 %all-to-all-start.7 = ((bf16[4,2,320,320]{2,1,3,0:T(2,128)(2,1)}), bf16[4,2,320,320]{2,1,3,0:T(2,128)(2,1)S(1)}, u32[]{:S(2)}, u32[]{:S(2)}) async-start(bf16[4,2,320,320]{2,1,3,0:T(2,128)(2,1)} %bitcast.105), calls=%async_computation.7 | async-start | bytes 3932160 | tf_op jit(solution)/shard_map/all_to_all | solution.py:22
  109.4 4.8 %convolution_convert_fusion.3 = bf16[64,1024]{1,0:T(8,128)(2,1)} fusion(bf16[1024,2560]{1,0:T(8,128)(2,1)} %param.6, bf16[8,8,2560]{2,1,0:T(8,128)(2,1)S(1)} %all-to-all-done), kind=kOutput, calls=%fused_computation.19 | convolution fusion | flops 335609856 | bytes 5701632 | tf_op jit(solution)/shard_map/dot_general | solution.py:18
  114.3 15.9 %all-to-all-done.7 = bf16[4,2,320,320]{2,1,3,0:T(2,128)(2,1)S(1)} async-done(((bf16[4,2,320,320]{2,1,3,0:T(2,128)(2,1)}), bf16[4,2,320,320]{2,1,3,0:T(2,128)(2,1)S(1)}, u32[]{:S(2)}, u32[]{:S(2)}) %all-to-all-start.7) | async-done | bytes 1638432 | tf_op jit(solution)/shard_map/all_to_all | solution.py:22
  130.1 5.3 %copy.122 = bf16[4,2,320,320]{3,2,1,0:T(8,128)(2,1)} copy(bf16[4,2,320,320]{2,1,3,0:T(2,128)(2,1)S(1)} %all-to-all-done.7) | data formatting | bytes 3276800 | tf_op jit(solution)/shard_map/all_to_all | solution.py:22
  138.8 18.5 %collective-permute-done.3 = bf16[320,320]{1,0:T(8,128)(2,1)S(1)} collective-permute-done((bf16[320,320]{1,0:T(8,128)(2,1)S(1)}, bf16[320,320]{1,0:T(8,128)(2,1)S(1)}, u32[]{:S(2)}, u32[]{:S(2)}) %collective-permute-start.3) | collective-permute-done | bytes 204832 | tf_op jit(solution)/shard_map/ppermute | solution.py:36
  159.5 12.6 %collective-permute-done.4 = bf16[320,320]{1,0:T(8,128)(2,1)S(1)} collective-permute-done((bf16[320,320]{1,0:T(8,128)(2,1)S(1)}, bf16[320,320]{1,0:T(8,128)(2,1)S(1)}, u32[]{:S(2)}, u32[]{:S(2)}) %collective-permute-start.4) | collective-permute-done | bytes 204832 | tf_op jit(solution)/shard_map/ppermute | solution.py:41
  178.8 5.7 %convolution_convert_fusion.1 = bf16[2048,320]{0,1:T(8,128)(2,1)} fusion(bf16[320,1024]{1,0:T(8,128)(2,1)S(1)} %copy-done.7, bf16[1024,1024]{1,0:T(8,128)(2,1)} %collective-permute-done, bf16[1024,1024]{1,0:T(8,128)(2,1)} %bitcast.13, pred[]{:T(512)S(6)} %eq.13), kind=kOutput, calls=%fused_computation.4 | convolution fusion | flops 1361707008 | bytes 6160385 | tf_op jit(solution)/shard_map/dot_general | solution.py:18
  189.8 7.6 %all-to-all-done.8 = bf16[4,2,320,320]{2,3,1,0:T(8,128)(2,1)S(1)} async-done(((bf16[4,2,320,320]{2,3,1,0:T(8,128)(2,1)}), bf16[4,2,320,320]{2,3,1,0:T(8,128)(2,1)S(1)}, u32[]{:S(2)}, u32[]{:S(2)}) %all-to-all-start.8) | async-done | bytes 1638432 | tf_op jit(solution)/shard_map/all_to_all | solution.py:22
  197.4 5.6 %all-to-all-start.5 = ((bf16[4,2,256,320]{2,1,3,0:T(2,128)(2,1)}), bf16[4,2,256,320]{2,1,3,0:T(2,128)(2,1)S(1)}, u32[]{:S(2)}, u32[]{:S(2)}) async-start(bf16[4,2,256,320]{2,1,3,0:T(2,128)(2,1)} %bitcast.100), calls=%async_computation.5 | async-start | bytes 2621440 | tf_op jit(solution)/shard_map/all_to_all | solution.py:22
  214.3 6.7 %collective-permute-start.1 = (bf16[256,320]{0,1:T(8,128)(2,1)S(1)}, bf16[256,320]{0,1:T(8,128)(2,1)S(1)}, u32[]{:S(2)}, u32[]{:S(2)}) collective-permute-start(bf16[256,320]{0,1:T(8,128)(2,1)S(1)} %fusion.14), channel_id=1, source_target_pairs={{0,128},{32,160},{64,192},{96,224},{128,0},{160,32},{192,64},{224,... | collective-permute-start | bytes 491528 | tf_op jit(solution)/shard_map/ppermute | solution.py:36
  227.2 6.3 %all-to-all-start.11 = ((bf16[4,2,256,320]{2,1,3,0:T(2,128)(2,1)}), bf16[4,2,256,320]{2,1,3,0:T(2,128)(2,1)}, u32[]{:S(2)}, u32[]{:S(2)}) async-start(bf16[4,2,256,320]{2,1,3,0:T(2,128)(2,1)} %broadcast_in_dim.63), calls=%async_computation.11 | async-start | bytes 2621440 | tf_op jit(solution)/shard_map/all_to_all | solution.py:22
  239.2 6.0 %all-to-all-done.11 = bf16[4,2,256,320]{2,1,3,0:T(2,128)(2,1)} async-done(((bf16[4,2,256,320]{2,1,3,0:T(2,128)(2,1)}), bf16[4,2,256,320]{2,1,3,0:T(2,128)(2,1)}, u32[]{:S(2)}, u32[]{:S(2)}) %all-to-all-start.11) | async-done | bytes 1310752 | tf_op jit(solution)/shard_map/all_to_all | solution.py:22
  254.2 6.4 %collective-permute-done.2 = bf16[256,320]{0,1:T(8,128)(2,1)S(1)} collective-permute-done((bf16[256,320]{0,1:T(8,128)(2,1)S(1)}, bf16[256,320]{0,1:T(8,128)(2,1)S(1)}, u32[]{:S(2)}, u32[]{:S(2)}) %collective-permute-start.2) | collective-permute-done | bytes 163872 | tf_op jit(solution)/shard_map/ppermute | solution.py:41
  261.8 5.6 %all-to-all-start.6 = ((bf16[4,2,256,320]{2,3,1,0:T(8,128)(2,1)}), bf16[4,2,256,320]{2,3,1,0:T(8,128)(2,1)S(1)}, u32[]{:S(2)}, u32[]{:S(2)}) async-start(bf16[4,2,256,320]{2,3,1,0:T(8,128)(2,1)} %broadcast_in_dim.61), calls=%async_computation.6 | async-start | bytes 2621440 | tf_op jit(solution)/shard_map/all_to_all | solution.py:22
  277.6 9.5 %all-to-all-start.10 = ((f32[4,80,256]{2,1,0:T(8,128)}), f32[4,80,256]{2,1,0:T(8,128)S(1)}, u32[]{:S(2)}, u32[]{:S(2)}) async-start(f32[4,80,256]{2,1,0:T(8,128)} %convert_reduce_fusion.2), calls=%async_computation.10 | async-start | bytes 655360 | tf_op jit(solution)/shard_map/all_to_all | solution.py:22
  287.1 6.5 %fusion.10 = f32[320,1024]{1,0:T(8,128)} fusion(bf16[2048,320]{0,1:T(8,128)(2,1)} %reshape.170, bf16[1024,1024]{1,0:T(8,128)(2,1)} %collective-permute-done, bf16[1024,1024]{1,0:T(8,128)(2,1)} %bitcast.13, pred[]{:T(512)S(6)} %eq.13), kind=kOutput, calls=%fused_computation.20 | convolution fusion | flops 1361051648 | bytes 6815745 | tf_op jit(solution)/shard_map/dot_general | solution.py:18
  (83 shorter events, 90.9 us)
Async XLA Ops:
  7.2 11.9 %copy-start.5 = (bf16[2560,256]{1,0:T(8,128)(2,1)S(1)}, bf16[2560,256]{1,0:T(8,128)(2,1)}, u32[]{:S(2)}) copy-start(bf16[2560,256]{1,0:T(8,128)(2,1)} %param.10) | copy-start | bytes 3932164
  9.2 17.9 %all-to-all-start.1 = ((bf16[32,16,256]{2,1,0:T(8,128)(2,1)}), bf16[32,16,256]{2,1,0:T(8,128)(2,1)S(1)}, u32[]{:S(2)}, u32[]{:S(2)}) async-start(bf16[32,16,256]{2,1,0:T(8,128)(2,1)} %bitcast.7), calls=%async_computation.1 | async-start | bytes 524288 | tf_op jit(solution)/shard_map/all_to_all | solution.py:22
  28.4 8.8 %all-to-all-start.2 = ((bf16[4,4,16,256]{3,2,1,0:T(8,128)(2,1)}), bf16[4,4,16,256]{3,2,1,0:T(8,128)(2,1)S(1)}, u32[]{:S(2)}, u32[]{:S(2)}) async-start(bf16[4,4,16,256]{3,2,1,0:T(8,128)(2,1)} %fusion.16), calls=%async_computation.2 | async-start | bytes 262144 | tf_op jit(solution)/shard_map/all_to_all | solution.py:22
  38.0 19.0 %all-to-all-start = ((bf16[8,8,2560]{2,1,0:T(8,128)(2,1)}), bf16[8,8,2560]{2,1,0:T(8,128)(2,1)S(1)}, u32[]{:S(2)}, u32[]{:S(2)}) async-start(bf16[8,8,2560]{2,1,0:T(8,128)(2,1)} %broadcast_in_dim.53), calls=%async_computation | async-start | bytes 655360 | tf_op jit(solution)/shard_map/all_to_all | solution.py:22
  72.7 8.2 %copy-start.6 = (bf16[1024,320]{0,1:T(8,128)(2,1)S(1)}, bf16[1024,320]{0,1:T(8,128)(2,1)}, u32[]{:S(2)}) copy-start(bf16[1024,320]{0,1:T(8,128)(2,1)} %param.7) | copy-start | bytes 1966084
  72.7 31.4 %all-to-all-start.4 = ((bf16[4,256,1024]{2,1,0:T(8,128)(2,1)}), bf16[4,256,1024]{2,1,0:T(8,128)(2,1)}, u32[]{:S(2)}, u32[]{:S(2)}) async-start(bf16[4,256,1024]{2,1,0:T(8,128)(2,1)} %broadcast_in_dim.60), calls=%async_computation.4 | async-start | bytes 4194304 | tf_op jit(solution)/shard_map/all_to_all | solution.py:22
  104.1 26.0 %all-to-all-start.7 = ((bf16[4,2,320,320]{2,1,3,0:T(2,128)(2,1)}), bf16[4,2,320,320]{2,1,3,0:T(2,128)(2,1)S(1)}, u32[]{:S(2)}, u32[]{:S(2)}) async-start(bf16[4,2,320,320]{2,1,3,0:T(2,128)(2,1)} %bitcast.105), calls=%async_computation.7 | async-start | bytes 3932160 | tf_op jit(solution)/shard_map/all_to_all | solution.py:22
  109.4 186.0 %all-gather.2.cloned.1.call-start = ((), (), s32[]{:S(2)}) async-start(), calls=%async_computation.12 | async-start | bytes 4325376 | tf_op jit(solution)/shard_map/all_gather | solution.py:78
  109.4 69.3 %collective-permute-start = (bf16[1024,1024]{1,0:T(8,128)(2,1)}, bf16[1024,1024]{1,0:T(8,128)(2,1)}, u32[]{:S(2)}, u32[]{:S(2)}) collective-permute-start(bf16[1024,1024]{1,0:T(8,128)(2,1)} %bitcast.13), channel_id=1, source_target_pairs={{0,1},{1,0},{2,3},{3,2},{4,5},{5,4},{6,7},{7,6},{8,9},{9,8},{10,11... | collective-permute-start | bytes 6291464 | tf_op jit(solution)/shard_map/ppermute | solution.py:59
  137.5 19.9 %collective-permute-start.3 = (bf16[320,320]{1,0:T(8,128)(2,1)S(1)}, bf16[320,320]{1,0:T(8,128)(2,1)S(1)}, u32[]{:S(2)}, u32[]{:S(2)}) collective-permute-start(bf16[320,320]{1,0:T(8,128)(2,1)S(1)} %fusion.20), channel_id=1, source_target_pairs={{0,128},{32,160},{64,192},{96,224},{128,0},{160,32},{192,64},{224,... | collective-permute-start | bytes 614408 | tf_op jit(solution)/shard_map/ppermute | solution.py:36
  158.2 14.0 %collective-permute-start.4 = (bf16[320,320]{1,0:T(8,128)(2,1)S(1)}, bf16[320,320]{1,0:T(8,128)(2,1)S(1)}, u32[]{:S(2)}, u32[]{:S(2)}) collective-permute-start(bf16[320,320]{1,0:T(8,128)(2,1)S(1)} %get-tuple-element.8), channel_id=1, source_target_pairs={{0,128},{32,160},{64,192},{96,224},{128,0},{160,32},{192,64},{224,... | collective-permute-start | bytes 614408 | tf_op jit(solution)/shard_map/ppermute | solution.py:41
  174.1 23.3 %all-to-all-start.8 = ((bf16[4,2,320,320]{2,3,1,0:T(8,128)(2,1)}), bf16[4,2,320,320]{2,3,1,0:T(8,128)(2,1)S(1)}, u32[]{:S(2)}, u32[]{:S(2)}) async-start(bf16[4,2,320,320]{2,3,1,0:T(8,128)(2,1)} %broadcast_in_dim.62), calls=%async_computation.8 | async-start | bytes 3932160 | tf_op jit(solution)/shard_map/all_to_all | solution.py:22
  197.4 23.7 %copy-start.2 = (bf16[4,2,320,320]{2,3,1,0:T(8,128)(2,1)}, bf16[4,2,320,320]{2,3,1,0:T(8,128)(2,1)S(1)}, u32[]{:S(2)}) copy-start(bf16[4,2,320,320]{2,3,1,0:T(8,128)(2,1)S(1)} %all-to-all-done.8) | copy-start | bytes 4915204
  197.4 16.0 %all-to-all-start.5 = ((bf16[4,2,256,320]{2,1,3,0:T(2,128)(2,1)}), bf16[4,2,256,320]{2,1,3,0:T(2,128)(2,1)S(1)}, u32[]{:S(2)}, u32[]{:S(2)}) async-start(bf16[4,2,256,320]{2,1,3,0:T(2,128)(2,1)} %bitcast.100), calls=%async_computation.5 | async-start | bytes 2621440 | tf_op jit(solution)/shard_map/all_to_all | solution.py:22
  204.9 19.1 %collective-permute-start.6 = (bf16[256,320]{0,1:T(8,128)(2,1)S(1)}, bf16[256,320]{0,1:T(8,128)(2,1)}, u32[]{:S(2)}, u32[]{:S(2)}) collective-permute-start(bf16[256,320]{0,1:T(8,128)(2,1)S(1)} %bitcast.119), channel_id=1, source_target_pairs={{0,128},{32,160},{64,192},{96,224},{128,0},{160,32},{192,64},{224,... | collective-permute-start | bytes 491528 | tf_op jit(solution)/shard_map/ppermute | solution.py:41
  214.3 19.1 %collective-permute-start.1 = (bf16[256,320]{0,1:T(8,128)(2,1)S(1)}, bf16[256,320]{0,1:T(8,128)(2,1)S(1)}, u32[]{:S(2)}, u32[]{:S(2)}) collective-permute-start(bf16[256,320]{0,1:T(8,128)(2,1)S(1)} %fusion.14), channel_id=1, source_target_pairs={{0,128},{32,160},{64,192},{96,224},{128,0},{160,32},{192,64},{224,... | collective-permute-start | bytes 491528 | tf_op jit(solution)/shard_map/ppermute | solution.py:36
  225.4 8.1 %copy-start.4 = (f32[2,256,320]{1,2,0:T(8,128)S(1)}, f32[2,256,320]{1,2,0:T(8,128)}, u32[]{:S(2)}) copy-start(f32[2,256,320]{1,2,0:T(8,128)} %copy-done.3) | copy-start | bytes 1966084
  227.2 18.0 %all-to-all-start.11 = ((bf16[4,2,256,320]{2,1,3,0:T(2,128)(2,1)}), bf16[4,2,256,320]{2,1,3,0:T(2,128)(2,1)}, u32[]{:S(2)}, u32[]{:S(2)}) async-start(bf16[4,2,256,320]{2,1,3,0:T(2,128)(2,1)} %broadcast_in_dim.63), calls=%async_computation.11 | async-start | bytes 2621440 | tf_op jit(solution)/shard_map/all_to_all | solution.py:22
  234.8 2.3 collective-permute-start.5
  245.1 15.5 %all-to-all-start.9 = ((bf16[4,4,80,256]{3,2,1,0:T(8,128)(2,1)}), bf16[4,4,80,256]{3,2,1,0:T(8,128)(2,1)S(1)}, u32[]{:S(2)}, u32[]{:S(2)}) async-start(bf16[4,4,80,256]{3,2,1,0:T(8,128)(2,1)} %bitcast.107), calls=%async_computation.9 | async-start | bytes 1310720 | tf_op jit(solution)/shard_map/all_to_all | solution.py:22
  249.6 11.0 %collective-permute-start.2 = (bf16[256,320]{0,1:T(8,128)(2,1)S(1)}, bf16[256,320]{0,1:T(8,128)(2,1)S(1)}, u32[]{:S(2)}, u32[]{:S(2)}) collective-permute-start(bf16[256,320]{0,1:T(8,128)(2,1)S(1)} %fusion.12), channel_id=1, source_target_pairs={{0,128},{32,160},{64,192},{96,224},{128,0},{160,32},{192,64},{224,... | collective-permute-start | bytes 491528 | tf_op jit(solution)/shard_map/ppermute | solution.py:41
  261.8 15.8 %all-to-all-start.6 = ((bf16[4,2,256,320]{2,3,1,0:T(8,128)(2,1)}), bf16[4,2,256,320]{2,3,1,0:T(8,128)(2,1)S(1)}, u32[]{:S(2)}, u32[]{:S(2)}) async-start(bf16[4,2,256,320]{2,3,1,0:T(8,128)(2,1)} %broadcast_in_dim.61), calls=%async_computation.6 | async-start | bytes 2621440 | tf_op jit(solution)/shard_map/all_to_all | solution.py:22
  277.6 17.1 %all-to-all-start.10 = ((f32[4,80,256]{2,1,0:T(8,128)}), f32[4,80,256]{2,1,0:T(8,128)S(1)}, u32[]{:S(2)}, u32[]{:S(2)}) async-start(f32[4,80,256]{2,1,0:T(8,128)} %convert_reduce_fusion.2), calls=%async_computation.10 | async-start | bytes 655360 | tf_op jit(solution)/shard_map/all_to_all | solution.py:22
  295.4 4.7 %copy-start.1 = (bf16[2048,256]{1,0:T(8,128)(2,1)S(1)}, bf16[2048,256]{1,0:T(8,128)(2,1)}, u32[]{:S(2)}) copy-start(bf16[2048,256]{1,0:T(8,128)(2,1)} %param.8) | copy-start | bytes 3145732
  (3 other events, 6.7 us)
Sparse Core Ops, SparseCore 0:
  114.4 78.4 all-gather.1
